TPU v7x, 512 devices: a whole 4x8x8 slice. The times are simulated.
512 devices in a mesh: row: 16 (over y_hi, x, core), col: 32 (over y_lo, z).
Axes of the slice: x: 4, y: 8 (y_hi: 2, y_lo: 4; y = y_hi * 4 + y_lo), z: 8, core: 2. Of those that a mesh axis runs over, the one named last changes fastest.
Arguments:
- ci_coeffs: float32 [8192, 8192], P('row', 'col'), may hold values from -6 to 6
- h_blocks: float32 [64, 24, 128, 128], P('col'), may hold values from -0.109375 to 0.109375
- block_columns: int32 [64, 24], P('col'), may hold values from 0 to 63, as said below
Outputs:
- sigma: float32 [8192, 8192], P('row', 'col')
Inputs may be any that keep to these rules, and one draw needn't show every extreme that they name: `block_columns`: block row J lists 24 different block columns, J itself among them, each of the form (J + t) modulo 64 with -16 <= t < 16.
All inputs are finite; a program needn't handle non-finite values.
Results may differ from a plain program's by a relative error of at most 0.0001.
Values sent between devices are 32-bit elements; how exact they have to be, the bound alone decides.
A program may use at most 64 MiB of HBM per device.

v0:
```python
import jax
import jax.numpy as jnp
from jax import lax
from jax.sharding import PartitionSpec as P

HALF = 16


highest = lax.Precision.HIGHEST


def from_partner(block, axis, stride):
    count = lax.axis_size(axis)
    route = []
    for low in range(count):
        high = low | 1 << stride
        if high != low and high < count:
            route += [(low, high), (high, low)]
    return lax.ppermute(block, axis, route)


def from_behind(block, axis, distance):
    devices = range(lax.axis_size(axis))
    route = [((i - distance) % len(devices), i) for i in devices]
    return lax.ppermute(block, axis, route)


def place_blocks(h_blocks, block_columns, column_index, reach_devices):
    per_device = h_blocks.shape[0]
    block_size = h_blocks.shape[2]
    devices_col = lax.axis_size("col")
    holding = block_columns // per_device
    offset = (holding - column_index + devices_col // 2) % devices_col - devices_col // 2
    target_slot = offset + reach_devices
    within = block_columns % per_device
    slot_range = jnp.arange(2 * reach_devices + 1, dtype=jnp.int32)
    within_range = jnp.arange(per_device, dtype=jnp.int32)
    selector = (
        (target_slot[:, :, None, None] == slot_range[None, None, :, None])
        & (within[:, :, None, None] == within_range[None, None, None, :])
    ).astype(jnp.float32)
    placed = jnp.einsum("jksq,jkbe->jbsqe", selector, h_blocks, precision=highest)
    return placed.reshape(per_device * block_size, 2 * reach_devices + 1, per_device * block_size)


def mirror_step(halves, bit_number):
    return from_partner(halves, ("row", "col"), bit_number)


def local(ci_coeffs, h_blocks, block_columns):
    per_device = h_blocks.shape[0]
    devices_col = lax.axis_size("col")
    reach_devices = (HALF + per_device - 1) // per_device
    column_index = lax.axis_index("col")
    row_index = lax.axis_index("row")
    placed = place_blocks(h_blocks, block_columns, column_index, reach_devices)
    partial_value = jnp.einsum("rb,bsf->srf", ci_coeffs, placed, precision=highest)
    summed = partial_value[reach_devices]
    for distance in range(1, reach_devices + 1):
        for signed in (distance, -distance):
            summed = summed + from_behind(partial_value[reach_devices + signed], "col", signed)
    tile_rows, tile_cols = summed.shape
    halves = summed.reshape(2, tile_cols, tile_cols)
    joined = row_index * devices_col + column_index
    parity = column_index % 2
    outgoing = jnp.where(parity == 0, halves[1], halves[0])
    incoming = from_partner(outgoing, ("row", "col"), 0)
    halves = jnp.where(
        parity == 0, jnp.stack([halves[0], incoming]), jnp.stack([incoming, halves[1]])
    )
    row_bits = lax.axis_size("row").bit_length() - 1
    for position in range(row_bits):
        high_bit = row_bits + 1 + position
        low_bit = position + 1
        relocated = mirror_step(mirror_step(halves, high_bit), low_bit)
        differs = joined // 2**high_bit % 2 != joined // 2**low_bit % 2
        halves = jnp.where(differs, relocated, halves)
    mirrored = jnp.swapaxes(halves, 1, 2).reshape(tile_rows, tile_cols)
    return summed + mirrored


def solution(mesh):
    return jax.shard_map(
        local,
        mesh=mesh,
        in_specs=(P("row", "col"), P("col", None, None, None), P("col", None)),
        out_specs=P("row", "col"),
        check_vma=False,
    )
```

profile of v0, /device:TPU:1, one launch (start us, length us, event | category | flops | bytes accessed | tf_op | source)
XLA Modules:
  0.0 480.6 jit_solution(2645615805703916040)
XLA Ops:
  1.9 4.9 %fusion.2 = f32[2,128,17,2,128]{4,2,1,3,0:T(8,128)S(1)} fusion(f32[2,24,128,128,1]{3,2,1,0,4:T(8,128)S(1)} %bitcast.90, pred[2,24,2]{1,2,0:T(4,128)(4,1)S(1)} %iota_compare_fusion.1, pred[2,24,17]{1,2,0:T(8,128)(4,1)S(1)} %iota_compare_fusion), kind=kOutput, calls=%fused_computation.3 | convolution fusion | flops 320865888 | bytes 7603088 | tf_op jit(solution)/shard_map/jksq,jkbe->jbsqe/dot_general | solution.py:42
  6.8 5.5 %copy.8 = f32[2,128,17,2,128]{4,3,1,0,2:T(2,128)} copy(f32[2,128,17,2,128]{4,2,1,3,0:T(8,128)S(1)} %fusion.2) | data formatting | bytes 8912896 | tf_op jit(solution)/shard_map/jksq,jkbe->jbsqe/transpose | solution.py:42
  12.3 6.7 %reshape.33 = f32[256,17,256]{2,0,1:T(8,128)} reshape(f32[2,128,17,2,128]{4,3,1,0,2:T(2,128)} %copy.8) | data formatting | bytes 8912896 | tf_op jit(solution)/shard_map/reshape | solution.py:43
  19.0 16.8 %convolution_bitcast_fusion = f32[17,512,256]{1,2,0:T(8,128)S(1)} fusion(f32[256,17,256]{2,0,1:T(8,128)} %reshape.33, f32[512,256]{1,0:T(8,128)} %param.3), kind=kOutput, calls=%fused_computation | convolution fusion | flops 6845104128 | bytes 13893632 | tf_op jit(solution)/shard_map/rb,bsf->srf/dot_general | solution.py:57
  35.8 2.7 slice_bitcast_fusion.15
  38.4 1.5 copy-done.1
  40.0 4.8 %collective-permute-start = (f32[512,256]{0,1:T(8,128)S(1)}, f32[512,256]{0,1:T(8,128)}, u32[]{:S(2)}, u32[]{:S(2)}) collective-permute-start(f32[512,256]{0,1:T(8,128)S(1)} %get-tuple-element.5), channel_id=1, source_target_pairs={{31,0},{0,1},{1,2},{2,3},{3,4},{4,5},{5,6},{6,7},{7,8},{8,9},{9,10... | collective-permute-start | bytes 1572872 | tf_op jit(solution)/shard_map/ppermute | solution.py:25
  44.8 11.6 %collective-permute-start.1 = (f32[512,256]{0,1:T(8,128)S(1)}, f32[512,256]{0,1:T(8,128)}, u32[]{:S(2)}, u32[]{:S(2)}) collective-permute-start(f32[512,256]{0,1:T(8,128)S(1)} %get-tuple-element.20), channel_id=1, source_target_pairs={{1,0},{2,1},{3,2},{4,3},{5,4},{6,5},{7,6},{8,7},{9,8},{10,9},{11,1... | collective-permute-start | bytes 1572872 | tf_op jit(solution)/shard_map/ppermute | solution.py:25
  56.4 1.9 collective-permute-start.10
  58.4 7.0 %collective-permute-start.11 = (f32[512,256]{0,1:T(8,128)S(1)}, f32[512,256]{0,1:T(8,128)}, u32[]{:S(2)}, u32[]{:S(2)}) collective-permute-start(f32[512,256]{0,1:T(8,128)S(1)} %get-tuple-element.10), channel_id=1, source_target_pairs={{6,0},{7,1},{8,2},{9,3},{10,4},{11,5},{12,6},{13,7},{14,8},{15,9},... | collective-permute-start | bytes 1572872 | tf_op jit(solution)/shard_map/ppermute | solution.py:25
  65.3 1.9 collective-permute-start.12
  67.3 6.1 %collective-permute-start.13 = (f32[512,256]{0,1:T(8,128)S(1)}, f32[512,256]{0,1:T(8,128)}, u32[]{:S(2)}, u32[]{:S(2)}) collective-permute-start(f32[512,256]{0,1:T(8,128)S(1)} %get-tuple-element.8), channel_id=1, source_target_pairs={{7,0},{8,1},{9,2},{10,3},{11,4},{12,5},{13,6},{14,7},{15,8},{16,9}... | collective-permute-start | bytes 1572872 | tf_op jit(solution)/shard_map/ppermute | solution.py:25
  73.3 1.9 collective-permute-start.14
  75.3 17.6 %collective-permute-done.10 = f32[512,256]{0,1:T(8,128)} collective-permute-done((f32[512,256]{0,1:T(8,128)S(1)}, f32[512,256]{0,1:T(8,128)}, u32[]{:S(2)}, u32[]{:S(2)}) %collective-permute-start.10) | collective-permute-done | bytes 524320 | tf_op jit(solution)/shard_map/ppermute | solution.py:25
  92.8 7.0 %collective-permute-start.15 = (f32[512,256]{0,1:T(8,128)S(1)}, f32[512,256]{0,1:T(8,128)}, u32[]{:S(2)}, u32[]{:S(2)}) collective-permute-start(f32[512,256]{0,1:T(8,128)S(1)} %get-tuple-element.6), channel_id=1, source_target_pairs={{8,0},{9,1},{10,2},{11,3},{12,4},{13,5},{14,6},{15,7},{16,8},{17,9... | collective-permute-start | bytes 1572872 | tf_op jit(solution)/shard_map/ppermute | solution.py:25
  99.9 8.3 %collective-permute-start.2 = (f32[512,256]{0,1:T(8,128)S(1)}, f32[512,256]{0,1:T(8,128)}, u32[]{:S(2)}, u32[]{:S(2)}) collective-permute-start(f32[512,256]{0,1:T(8,128)S(1)} %get-tuple-element.19), channel_id=1, source_target_pairs={{30,0},{31,1},{0,2},{1,3},{2,4},{3,5},{4,6},{5,7},{6,8},{7,9},{8,1... | collective-permute-start | bytes 1572872 | tf_op jit(solution)/shard_map/ppermute | solution.py:25
  108.1 2.8 collective-permute-start.3
  111.0 5.4 %collective-permute-start.4 = (f32[512,256]{0,1:T(8,128)S(1)}, f32[512,256]{0,1:T(8,128)S(1)}, u32[]{:S(2)}, u32[]{:S(2)}) collective-permute-start(f32[512,256]{0,1:T(8,128)S(1)} %get-tuple-element.17), channel_id=1, source_target_pairs={{29,0},{30,1},{31,2},{0,3},{1,4},{2,5},{3,6},{4,7},{5,8},{6,9},{7,... | collective-permute-start | bytes 1572872 | tf_op jit(solution)/shard_map/ppermute | solution.py:25
  116.4 15.2 %collective-permute-start.5 = (f32[512,256]{0,1:T(8,128)}, f32[512,256]{0,1:T(8,128)}, u32[]{:S(2)}, u32[]{:S(2)}) collective-permute-start(f32[512,256]{0,1:T(8,128)} %get-tuple-element.16), channel_id=1, source_target_pairs={{3,0},{4,1},{5,2},{6,3},{7,4},{8,5},{9,6},{10,7},{11,8},{12,9},{13... | collective-permute-start | bytes 1572872 | tf_op jit(solution)/shard_map/ppermute | solution.py:25
  131.7 12.2 %collective-permute-start.6 = (f32[512,256]{0,1:T(8,128)}, f32[512,256]{0,1:T(8,128)}, u32[]{:S(2)}, u32[]{:S(2)}) collective-permute-start(f32[512,256]{0,1:T(8,128)} %get-tuple-element.15), channel_id=1, source_target_pairs={{28,0},{29,1},{30,2},{31,3},{0,4},{1,5},{2,6},{3,7},{4,8},{5,9},{6... | collective-permute-start | bytes 1572872 | tf_op jit(solution)/shard_map/ppermute | solution.py:25
  143.9 10.8 %collective-permute-done.2 = f32[512,256]{0,1:T(8,128)} collective-permute-done((f32[512,256]{0,1:T(8,128)S(1)}, f32[512,256]{0,1:T(8,128)}, u32[]{:S(2)}, u32[]{:S(2)}) %collective-permute-start.2) | collective-permute-done | bytes 524320 | tf_op jit(solution)/shard_map/ppermute | solution.py:25
  154.7 54.2 %collective-permute-start.7 = (f32[512,256]{0,1:T(8,128)}, f32[512,256]{0,1:T(8,128)}, u32[]{:S(2)}, u32[]{:S(2)}) collective-permute-start(f32[512,256]{0,1:T(8,128)} %get-tuple-element.14), channel_id=1, source_target_pairs={{4,0},{5,1},{6,2},{7,3},{8,4},{9,5},{10,6},{11,7},{12,8},{13,9},{1... | collective-permute-start | bytes 1572872 | tf_op jit(solution)/shard_map/ppermute | solution.py:25
  208.9 27.1 %collective-permute-start.8 = (f32[512,256]{0,1:T(8,128)}, f32[512,256]{0,1:T(8,128)}, u32[]{:S(2)}, u32[]{:S(2)}) collective-permute-start(f32[512,256]{0,1:T(8,128)} %get-tuple-element.13), channel_id=1, source_target_pairs={{27,0},{28,1},{29,2},{30,3},{31,4},{0,5},{1,6},{2,7},{3,8},{4,9},{... | collective-permute-start | bytes 1572872 | tf_op jit(solution)/shard_map/ppermute | solution.py:25
  236.8 2.1 collective-permute-start.9
  239.0 51.1 %collective-permute-done.8 = f32[512,256]{0,1:T(8,128)} collective-permute-done((f32[512,256]{0,1:T(8,128)}, f32[512,256]{0,1:T(8,128)}, u32[]{:S(2)}, u32[]{:S(2)}) %collective-permute-start.8) | collective-permute-done | bytes 524320 | tf_op jit(solution)/shard_map/ppermute | solution.py:25
  290.2 4.6 fusion.20
  295.6 1.9 collective-permute-start.16
  297.6 7.3 %collective-permute-done.16 = f32[256,256]{0,1:T(8,128)S(1)} collective-permute-done((f32[256,256]{0,1:T(8,128)S(1)}, f32[256,256]{0,1:T(8,128)S(1)}, u32[]{:S(2)}, u32[]{:S(2)}) %collective-permute-start.16) | collective-permute-done | bytes 262176 | tf_op jit(solution)/shard_map/ppermute | solution.py:19
  305.6 3.2 collective-permute-start.17
  308.9 1.6 collective-permute-done.17
  310.5 8.2 %collective-permute-start.18 = (f32[2,256,256]{1,2,0:T(8,128)}, f32[2,256,256]{1,2,0:T(8,128)}, u32[]{:S(2)}, u32[]{:S(2)}) collective-permute-start(f32[2,256,256]{1,2,0:T(8,128)} %collective-permute-done.17), channel_id=1, source_target_pairs={{0,2},{2,0},{1,3},{3,1},{4,6},{6,4},{5,7},{7,5},{8,10},{10,8},{9,1... | collective-permute-start | bytes 1572872 | tf_op jit(solution)/shard_map/ppermute | solution.py:19
  318.8 23.5 %collective-permute-done.18 = f32[2,256,256]{1,2,0:T(8,128)} collective-permute-done((f32[2,256,256]{1,2,0:T(8,128)}, f32[2,256,256]{1,2,0:T(8,128)}, u32[]{:S(2)}, u32[]{:S(2)}) %collective-permute-start.18) | collective-permute-done | bytes 524320 | tf_op jit(solution)/shard_map/ppermute | solution.py:19
  344.4 1.9 collective-permute-start.19
  346.3 12.8 %collective-permute-done.19 = f32[2,256,256]{1,2,0:T(8,128)} collective-permute-done((f32[2,256,256]{1,2,0:T(8,128)S(1)}, f32[2,256,256]{1,2,0:T(8,128)}, u32[]{:S(2)}, u32[]{:S(2)}) %collective-permute-start.19) | collective-permute-done | bytes 524320 | tf_op jit(solution)/shard_map/ppermute | solution.py:19
  359.1 2.2 collective-permute-start.20
  361.4 24.1 %collective-permute-done.20 = f32[2,256,256]{1,2,0:T(8,128)} collective-permute-done((f32[2,256,256]{1,2,0:T(8,128)}, f32[2,256,256]{1,2,0:T(8,128)}, u32[]{:S(2)}, u32[]{:S(2)}) %collective-permute-start.20) | collective-permute-done | bytes 524320 | tf_op jit(solution)/shard_map/ppermute | solution.py:19
  387.4 4.7 collective-permute-start.21
  392.1 10.0 %collective-permute-done.21 = f32[2,256,256]{1,2,0:T(8,128)} collective-permute-done((f32[2,256,256]{1,2,0:T(8,128)S(1)}, f32[2,256,256]{1,2,0:T(8,128)}, u32[]{:S(2)}, u32[]{:S(2)}) %collective-permute-start.21) | collective-permute-done | bytes 524320 | tf_op jit(solution)/shard_map/ppermute | solution.py:19
  402.1 1.9 collective-permute-start.22
  404.1 10.6 %collective-permute-done.22 = f32[2,256,256]{1,2,0:T(8,128)} collective-permute-done((f32[2,256,256]{1,2,0:T(8,128)}, f32[2,256,256]{1,2,0:T(8,128)}, u32[]{:S(2)}, u32[]{:S(2)}) %collective-permute-start.22) | collective-permute-done | bytes 524320 | tf_op jit(solution)/shard_map/ppermute | solution.py:19
  416.6 1.9 collective-permute-start.23
  418.5 15.0 %collective-permute-done.23 = f32[2,256,256]{1,2,0:T(8,128)} collective-permute-done((f32[2,256,256]{1,2,0:T(8,128)S(1)}, f32[2,256,256]{1,2,0:T(8,128)}, u32[]{:S(2)}, u32[]{:S(2)}) %collective-permute-start.23) | collective-permute-done | bytes 524320 | tf_op jit(solution)/shard_map/ppermute | solution.py:19
  433.5 15.6 %collective-permute-start.24 = (f32[2,256,256]{1,2,0:T(8,128)}, f32[2,256,256]{1,2,0:T(8,128)}, u32[]{:S(2)}, u32[]{:S(2)}) collective-permute-start(f32[2,256,256]{1,2,0:T(8,128)} %collective-permute-done.23), channel_id=1, source_target_pairs={{0,16},{16,0},{1,17},{17,1},{2,18},{18,2},{3,19},{19,3},{4,20},{20... | collective-permute-start | bytes 1572872 | tf_op jit(solution)/shard_map/ppermute | solution.py:19
  449.2 23.4 %collective-permute-done.24 = f32[2,256,256]{1,2,0:T(8,128)} collective-permute-done((f32[2,256,256]{1,2,0:T(8,128)}, f32[2,256,256]{1,2,0:T(8,128)}, u32[]{:S(2)}, u32[]{:S(2)}) %collective-permute-start.24) | collective-permute-done | bytes 524320 | tf_op jit(solution)/shard_map/ppermute | solution.py:19
  472.6 1.9 broadcast_select_fusion.3
  474.5 2.0 copy.18
  476.5 2.1 add.144
  478.6 2.0 copy.11
  (40 shorter events, 10.2 us)
Async XLA Ops:
  0.0 1.9 copy-start
  35.8 4.2 copy-start.1
  40.0 27.3 %collective-permute-start = (f32[512,256]{0,1:T(8,128)S(1)}, f32[512,256]{0,1:T(8,128)}, u32[]{:S(2)}, u32[]{:S(2)}) collective-permute-start(f32[512,256]{0,1:T(8,128)S(1)} %get-tuple-element.5), channel_id=1, source_target_pairs={{31,0},{0,1},{1,2},{2,3},{3,4},{4,5},{5,6},{6,7},{7,8},{8,9},{9,10... | collective-permute-start | bytes 1572872 | tf_op jit(solution)/shard_map/ppermute | solution.py:25
  44.8 28.5 %collective-permute-start.1 = (f32[512,256]{0,1:T(8,128)S(1)}, f32[512,256]{0,1:T(8,128)}, u32[]{:S(2)}, u32[]{:S(2)}) collective-permute-start(f32[512,256]{0,1:T(8,128)S(1)} %get-tuple-element.20), channel_id=1, source_target_pairs={{1,0},{2,1},{3,2},{4,3},{5,4},{6,5},{7,6},{8,7},{9,8},{10,9},{11,1... | collective-permute-start | bytes 1572872 | tf_op jit(solution)/shard_map/ppermute | solution.py:25
  56.4 36.4 %collective-permute-start.10 = (f32[512,256]{0,1:T(8,128)S(1)}, f32[512,256]{0,1:T(8,128)}, u32[]{:S(2)}, u32[]{:S(2)}) collective-permute-start(f32[512,256]{0,1:T(8,128)S(1)} %get-tuple-element.11), channel_id=1, source_target_pairs={{26,0},{27,1},{28,2},{29,3},{30,4},{31,5},{0,6},{1,7},{2,8},{3,9},... | collective-permute-start | bytes 1572872 | tf_op jit(solution)/shard_map/ppermute | solution.py:25
  58.4 41.5 %collective-permute-start.11 = (f32[512,256]{0,1:T(8,128)S(1)}, f32[512,256]{0,1:T(8,128)}, u32[]{:S(2)}, u32[]{:S(2)}) collective-permute-start(f32[512,256]{0,1:T(8,128)S(1)} %get-tuple-element.10), channel_id=1, source_target_pairs={{6,0},{7,1},{8,2},{9,3},{10,4},{11,5},{12,6},{13,7},{14,8},{15,9},... | collective-permute-start | bytes 1572872 | tf_op jit(solution)/shard_map/ppermute | solution.py:25
  65.3 42.8 %collective-permute-start.12 = (f32[512,256]{0,1:T(8,128)S(1)}, f32[512,256]{0,1:T(8,128)}, u32[]{:S(2)}, u32[]{:S(2)}) collective-permute-start(f32[512,256]{0,1:T(8,128)S(1)} %get-tuple-element.9), channel_id=1, source_target_pairs={{25,0},{26,1},{27,2},{28,3},{29,4},{30,5},{31,6},{0,7},{1,8},{2,9}... | collective-permute-start | bytes 1572872 | tf_op jit(solution)/shard_map/ppermute | solution.py:25
  67.3 43.7 %collective-permute-start.13 = (f32[512,256]{0,1:T(8,128)S(1)}, f32[512,256]{0,1:T(8,128)}, u32[]{:S(2)}, u32[]{:S(2)}) collective-permute-start(f32[512,256]{0,1:T(8,128)S(1)} %get-tuple-element.8), channel_id=1, source_target_pairs={{7,0},{8,1},{9,2},{10,3},{11,4},{12,5},{13,6},{14,7},{15,8},{16,9}... | collective-permute-start | bytes 1572872 | tf_op jit(solution)/shard_map/ppermute | solution.py:25
  73.3 43.1 %collective-permute-start.14 = (f32[512,256]{0,1:T(8,128)S(1)}, f32[512,256]{0,1:T(8,128)}, u32[]{:S(2)}, u32[]{:S(2)}) collective-permute-start(f32[512,256]{0,1:T(8,128)S(1)} %get-tuple-element.7), channel_id=1, source_target_pairs={{24,0},{25,1},{26,2},{27,3},{28,4},{29,5},{30,6},{31,7},{0,8},{1,9... | collective-permute-start | bytes 1572872 | tf_op jit(solution)/shard_map/ppermute | solution.py:25
  92.8 38.8 %collective-permute-start.15 = (f32[512,256]{0,1:T(8,128)S(1)}, f32[512,256]{0,1:T(8,128)}, u32[]{:S(2)}, u32[]{:S(2)}) collective-permute-start(f32[512,256]{0,1:T(8,128)S(1)} %get-tuple-element.6), channel_id=1, source_target_pairs={{8,0},{9,1},{10,2},{11,3},{12,4},{13,5},{14,6},{15,7},{16,8},{17,9... | collective-permute-start | bytes 1572872 | tf_op jit(solution)/shard_map/ppermute | solution.py:25
  99.9 54.8 %collective-permute-start.2 = (f32[512,256]{0,1:T(8,128)S(1)}, f32[512,256]{0,1:T(8,128)}, u32[]{:S(2)}, u32[]{:S(2)}) collective-permute-start(f32[512,256]{0,1:T(8,128)S(1)} %get-tuple-element.19), channel_id=1, source_target_pairs={{30,0},{31,1},{0,2},{1,3},{2,4},{3,5},{4,6},{5,7},{6,8},{7,9},{8,1... | collective-permute-start | bytes 1572872 | tf_op jit(solution)/shard_map/ppermute | solution.py:25
  108.1 100.7 %collective-permute-start.3 = (f32[512,256]{0,1:T(8,128)S(1)}, f32[512,256]{0,1:T(8,128)S(1)}, u32[]{:S(2)}, u32[]{:S(2)}) collective-permute-start(f32[512,256]{0,1:T(8,128)S(1)} %get-tuple-element.18), channel_id=1, source_target_pairs={{2,0},{3,1},{4,2},{5,3},{6,4},{7,5},{8,6},{9,7},{10,8},{11,9},{12,... | collective-permute-start | bytes 1572872 | tf_op jit(solution)/shard_map/ppermute | solution.py:25
  111.0 125.0 %collective-permute-start.4 = (f32[512,256]{0,1:T(8,128)S(1)}, f32[512,256]{0,1:T(8,128)S(1)}, u32[]{:S(2)}, u32[]{:S(2)}) collective-permute-start(f32[512,256]{0,1:T(8,128)S(1)} %get-tuple-element.17), channel_id=1, source_target_pairs={{29,0},{30,1},{31,2},{0,3},{1,4},{2,5},{3,6},{4,7},{5,8},{6,9},{7,... | collective-permute-start | bytes 1572872 | tf_op jit(solution)/shard_map/ppermute | solution.py:25
  116.4 122.6 %collective-permute-start.5 = (f32[512,256]{0,1:T(8,128)}, f32[512,256]{0,1:T(8,128)}, u32[]{:S(2)}, u32[]{:S(2)}) collective-permute-start(f32[512,256]{0,1:T(8,128)} %get-tuple-element.16), channel_id=1, source_target_pairs={{3,0},{4,1},{5,2},{6,3},{7,4},{8,5},{9,6},{10,7},{11,8},{12,9},{13... | collective-permute-start | bytes 1572872 | tf_op jit(solution)/shard_map/ppermute | solution.py:25
  131.7 107.3 %collective-permute-start.6 = (f32[512,256]{0,1:T(8,128)}, f32[512,256]{0,1:T(8,128)}, u32[]{:S(2)}, u32[]{:S(2)}) collective-permute-start(f32[512,256]{0,1:T(8,128)} %get-tuple-element.15), channel_id=1, source_target_pairs={{28,0},{29,1},{30,2},{31,3},{0,4},{1,5},{2,6},{3,7},{4,8},{5,9},{6... | collective-permute-start | bytes 1572872 | tf_op jit(solution)/shard_map/ppermute | solution.py:25
  154.7 84.4 %collective-permute-start.7 = (f32[512,256]{0,1:T(8,128)}, f32[512,256]{0,1:T(8,128)}, u32[]{:S(2)}, u32[]{:S(2)}) collective-permute-start(f32[512,256]{0,1:T(8,128)} %get-tuple-element.14), channel_id=1, source_target_pairs={{4,0},{5,1},{6,2},{7,3},{8,4},{9,5},{10,6},{11,7},{12,8},{13,9},{1... | collective-permute-start | bytes 1572872 | tf_op jit(solution)/shard_map/ppermute | solution.py:25
  208.9 27.1 %copy-start.8 = (f32[512,256]{0,1:T(8,128)}, f32[512,256]{0,1:T(8,128)S(1)}, u32[]{:S(2)}) copy-start(f32[512,256]{0,1:T(8,128)S(1)} %collective-permute-done.3) | copy-start | bytes 1572868
  208.9 81.3 %collective-permute-start.8 = (f32[512,256]{0,1:T(8,128)}, f32[512,256]{0,1:T(8,128)}, u32[]{:S(2)}, u32[]{:S(2)}) collective-permute-start(f32[512,256]{0,1:T(8,128)} %get-tuple-element.13), channel_id=1, source_target_pairs={{27,0},{28,1},{29,2},{30,3},{31,4},{0,5},{1,6},{2,7},{3,8},{4,9},{... | collective-permute-start | bytes 1572872 | tf_op jit(solution)/shard_map/ppermute | solution.py:25
  236.0 0.8 copy-start.9
  236.8 53.3 %collective-permute-start.9 = (f32[512,256]{0,1:T(8,128)}, f32[512,256]{0,1:T(8,128)}, u32[]{:S(2)}, u32[]{:S(2)}) collective-permute-start(f32[512,256]{0,1:T(8,128)} %get-tuple-element.12), channel_id=1, source_target_pairs={{5,0},{6,1},{7,2},{8,3},{9,4},{10,5},{11,6},{12,7},{13,8},{14,9},{... | collective-permute-start | bytes 1572872 | tf_op jit(solution)/shard_map/ppermute | solution.py:25
  294.8 0.8 copy-start.2
  295.6 9.3 %copy-start.3 = (f32[1,256,256]{1,2,0:T(8,128)}, f32[1,256,256]{1,2,0:T(8,128)S(1)}, u32[]{:S(2)}) copy-start(f32[1,256,256]{1,2,0:T(8,128)S(1)} %get-tuple-element.23) | copy-start | bytes 786436
  295.6 9.3 %collective-permute-start.16 = (f32[256,256]{0,1:T(8,128)S(1)}, f32[256,256]{0,1:T(8,128)S(1)}, u32[]{:S(2)}, u32[]{:S(2)}) collective-permute-start(f32[256,256]{0,1:T(8,128)S(1)} %get-tuple-element.22), channel_id=1, source_target_pairs={{0,1},{1,0},{2,3},{3,2},{4,5},{5,4},{6,7},{7,6},{8,9},{9,8},{10,11... | collective-permute-start | bytes 786440 | tf_op jit(solution)/shard_map/ppermute | solution.py:19
  304.9 0.7 copy-start.7
  305.6 4.9 %collective-permute-start.17 = (f32[2,256,256]{1,2,0:T(8,128)S(1)}, f32[2,256,256]{1,2,0:T(8,128)}, u32[]{:S(2)}, u32[]{:S(2)}) collective-permute-start(f32[2,256,256]{1,2,0:T(8,128)S(1)} %maximum_select_fusion), channel_id=1, source_target_pairs={{0,32},{32,0},{1,33},{33,1},{2,34},{34,2},{3,35},{35,3},{4,36},{36... | collective-permute-start | bytes 1572872 | tf_op jit(solution)/shard_map/ppermute | solution.py:19
  310.5 31.7 %collective-permute-start.18 = (f32[2,256,256]{1,2,0:T(8,128)}, f32[2,256,256]{1,2,0:T(8,128)}, u32[]{:S(2)}, u32[]{:S(2)}) collective-permute-start(f32[2,256,256]{1,2,0:T(8,128)} %collective-permute-done.17), channel_id=1, source_target_pairs={{0,2},{2,0},{1,3},{3,1},{4,6},{6,4},{5,7},{7,5},{8,10},{10,8},{9,1... | collective-permute-start | bytes 1572872 | tf_op jit(solution)/shard_map/ppermute | solution.py:19
  343.6 0.8 copy-start.4
  344.4 14.7 %collective-permute-start.19 = (f32[2,256,256]{1,2,0:T(8,128)S(1)}, f32[2,256,256]{1,2,0:T(8,128)}, u32[]{:S(2)}, u32[]{:S(2)}) collective-permute-start(f32[2,256,256]{1,2,0:T(8,128)S(1)} %broadcast_select_fusion), channel_id=1, source_target_pairs={{0,64},{64,0},{1,65},{65,1},{2,66},{66,2},{3,67},{67,3},{4,68},{68... | collective-permute-start | bytes 1572872 | tf_op jit(solution)/shard_map/ppermute | solution.py:19
  359.1 26.4 %collective-permute-start.20 = (f32[2,256,256]{1,2,0:T(8,128)}, f32[2,256,256]{1,2,0:T(8,128)}, u32[]{:S(2)}, u32[]{:S(2)}) collective-permute-start(f32[2,256,256]{1,2,0:T(8,128)} %collective-permute-done.19), channel_id=1, source_target_pairs={{0,4},{4,0},{1,5},{5,1},{2,6},{6,2},{3,7},{7,3},{8,12},{12,8},{9,1... | collective-permute-start | bytes 1572872 | tf_op jit(solution)/shard_map/ppermute | solution.py:19
  386.6 0.8 copy-start.6
  387.4 14.8 %collective-permute-start.21 = (f32[2,256,256]{1,2,0:T(8,128)S(1)}, f32[2,256,256]{1,2,0:T(8,128)}, u32[]{:S(2)}, u32[]{:S(2)}) collective-permute-start(f32[2,256,256]{1,2,0:T(8,128)S(1)} %broadcast_select_fusion.1), channel_id=1, source_target_pairs={{0,128},{128,0},{1,129},{129,1},{2,130},{130,2},{3,131},{131,3},{4... | collective-permute-start | bytes 1572872 | tf_op jit(solution)/shard_map/ppermute | solution.py:19
  402.1 12.5 %collective-permute-start.22 = (f32[2,256,256]{1,2,0:T(8,128)}, f32[2,256,256]{1,2,0:T(8,128)}, u32[]{:S(2)}, u32[]{:S(2)}) collective-permute-start(f32[2,256,256]{1,2,0:T(8,128)} %collective-permute-done.21), channel_id=1, source_target_pairs={{0,8},{8,0},{1,9},{9,1},{2,10},{10,2},{3,11},{11,3},{4,12},{12,4},... | collective-permute-start | bytes 1572872 | tf_op jit(solution)/shard_map/ppermute | solution.py:19
  415.8 0.8 copy-start.5
  416.6 17.0 %collective-permute-start.23 = (f32[2,256,256]{1,2,0:T(8,128)S(1)}, f32[2,256,256]{1,2,0:T(8,128)}, u32[]{:S(2)}, u32[]{:S(2)}) collective-permute-start(f32[2,256,256]{1,2,0:T(8,128)S(1)} %broadcast_select_fusion.2), channel_id=1, source_target_pairs={{0,256},{256,0},{1,257},{257,1},{2,258},{258,2},{3,259},{259,3},{4... | collective-permute-start | bytes 1572872 | tf_op jit(solution)/shard_map/ppermute | solution.py:19
  433.5 39.0 %collective-permute-start.24 = (f32[2,256,256]{1,2,0:T(8,128)}, f32[2,256,256]{1,2,0:T(8,128)}, u32[]{:S(2)}, u32[]{:S(2)}) collective-permute-start(f32[2,256,256]{1,2,0:T(8,128)} %collective-permute-done.23), channel_id=1, source_target_pairs={{0,16},{16,0},{1,17},{17,1},{2,18},{18,2},{3,19},{19,3},{4,20},{20... | collective-permute-start | bytes 1572872 | tf_op jit(solution)/shard_map/ppermute | solution.py:19
where the time goes:
time: 482 us; the launch traced here: 481 us
  starting transfers between devices  211 us (44%)
  waiting for transfers between devices  208 us (43%)
  local copies, waits for them, and re-layouts  26 us (5%)
  matrix products  21.7 us (5%)
  other arithmetic  13.1 us (3%)
    ppermute x16, starting transfers between devices, from_behind(): return lax.ppermute(block, axis, route)  170 us
    ppermute x9, waiting for transfers between devices, from_partner(): return lax.ppermute(block, axis, route)  128 us
    ppermute x16, waiting for transfers between devices, from_behind(): return lax.ppermute(block, axis, route)  79.5 us
    ppermute x9, starting transfers between devices, from_partner(): return lax.ppermute(block, axis, route)  41.5 us
    dot_general x1, matrix products, local(): jnp.einsum('rb,bsf->srf', ci_coeffs, placed, precision=highest)  16.8 us
  transfers between devices with their start and end apart: 25, of which 12 were waited for; matrix products, arithmetic and copies ran while one was open for 0% of the time, Pallas kernels for 0%

commit v1 on v0

v1 whole, which is shorter than its diff:
```python
import jax
import jax.numpy as jnp
from jax import lax
from jax.experimental import pallas as pl
from jax.experimental.pallas import tpu as pltpu
from jax.sharding import PartitionSpec as P

NX, NYL, NZ = 4, 4, 8
BS = 128
K = 24
CH = 4
ROWS = 512
COLS = 256
QR = ROWS // CH
OFFS = 36
MESH = pl.DeviceIdType.MESH
ORDER = (4, 3, 5, 2, 6, 1, 7, 0, 8)
STAGGER = 1


def split(value):
    high = value.astype(jnp.bfloat16)
    low = (value - high.astype(jnp.float32)).astype(jnp.bfloat16)
    return high, low


def dot(a, b):
    return jnp.dot(a, b, preferred_element_type=jnp.float32)


def kernel(
    where_ref, flag_ref, c_hbm, h_hbm, out_ref,
    cbuf, hraw, placed, hy, wown, wnear, xb, first, plus, minus, final, mirrored,
    loc_sem, yc_send, yc_recv, yh_send, yh_recv, xh_send, xh_recv, kh_send, kh_recv,
    zp_send, zp_recv, zm_send, zm_recv, m_send, m_recv,
):
    r = lax.axis_index("row")
    c = lax.axis_index("col")
    y_hi, x, core = r // 8, (r // 2) % NX, r % 2
    y_lo, z = c // NZ, c % NZ
    y = y_hi * NYL + y_lo

    def physical(step):
        other = (y + step + 2 * NYL) % (2 * NYL)
        return (other // NYL) * 8 + x * 2 + core, (other % NYL) * NZ + z

    def along_x(step):
        return y_hi * 8 + ((x + step) % NX) * 2 + core, c

    col_above = (r, ((y_lo + 1) % NYL) * NZ + z)
    col_below = (r, ((y_lo + NYL - 1) % NYL) * NZ + z)
    y_above, y_below = physical(1), physical(-1)
    z_above = (r, y_lo * NZ + (z + 1) % NZ)
    z_below = (r, y_lo * NZ + (z + NZ - 1) % NZ)
    sibling = (y_hi * 8 + x * 2 + 1 - core, c)
    peers = [along_x(step) for step in (1, 2, 3)]
    on_diagonal = (c // 2 == r).astype(jnp.int32)

    get_c = pltpu.make_async_copy(c_hbm, cbuf.at[0], loc_sem.at[0])
    get_h = pltpu.make_async_copy(h_hbm, hraw, loc_sem.at[1])
    get_c.start()
    get_h.start()

    barrier = pltpu.get_barrier_semaphore()
    fixed = [col_above, col_below, y_above, y_below, z_above, z_below, sibling] + peers
    for device in fixed:
        pl.semaphore_signal(barrier, inc=1, device_id=device, device_id_type=MESH)
    for half in range(2):
        @pl.when(jnp.logical_not((c // 2 == r) & (c % 2 == half)))
        def _():
            pl.semaphore_signal(barrier, inc=1, device_id=(c // 2, 2 * r + half), device_id_type=MESH)
    get_c.wait()
    get_h.wait()
    pl.semaphore_wait(barrier, len(fixed) + 2 - on_diagonal)

    sends = []

    def remote(src, dst, send_sem, recv_sem, device):
        copy = pltpu.make_async_remote_copy(
            src_ref=src, dst_ref=dst, send_sem=send_sem, recv_sem=recv_sem,
            device_id=device, device_id_type=MESH,
        )
        copy.start()
        sends.append(copy)

    def arrived(ref, sem):
        pltpu.make_async_copy(ref, ref, sem).wait()

    def rows(q):
        return pl.ds(q * QR, QR)

    def send_c(q):
        remote(cbuf.at[0, rows(q)], cbuf.at[2, rows(q)], yc_send.at[0, q], yc_recv.at[1, q], col_above)
        remote(cbuf.at[0, rows(q)], cbuf.at[1, rows(q)], yc_send.at[1, q], yc_recv.at[0, q], col_below)

    def place(index):
        for j in range(2):
            for e in range(2):
                at = 2 * (index - 8) + e - j + 17
                block = hraw[j, where_ref[j, at]] * flag_ref[j, at]
                placed[index, 2 * j:2 * j + 2, :, :, e * BS:(e + 1) * BS] = block.reshape(2, 2, 32, BS)

    def inside(d):
        return z + d < NZ

    def send_h(slot):
        if slot == 0:
            index, device = 0, y_below
        elif slot == 8:
            index, device = 16, y_above
        else:
            index = jnp.where(inside(slot), slot, slot + 8)
            device = tuple(jnp.where(inside(slot), b, a) for a, b in zip(y_above, y_below))
        remote(placed.at[index, x, core], hy.at[slot, x, core], yh_send.at[slot], yh_recv.at[slot], device)

    send_c(0)
    for slot in ORDER:
        if slot == 8:
            place(16)
        else:
            place(slot)
            place(slot + 8)
        send_h(slot)
    for q in range(1, CH):
        send_c(q)

    def spread_x(slot):
        arrived(hy.at[slot, x, core], yh_recv.at[slot])
        for step in range(3):
            remote(hy.at[slot, x, core], hy.at[slot, x, core], xh_send.at[slot, step], xh_recv.at[slot, step], peers[step])

    def spread_core(slot):
        for step in range(3):
            arrived(hy.at[slot, 0, 0], xh_recv.at[slot, step])
        remote(hy.at[slot, :, core], hy.at[slot, :, core], kh_send.at[slot], kh_recv.at[slot], sibling)

    def split_own(d):
        index = 8 if d == 0 else jnp.where(inside(d), d + 8, d)
        high, low = split(placed[index].reshape(COLS, COLS))
        wown[d, 0] = high
        wown[d, 1] = low

    def split_near(slot):
        arrived(hy.at[slot, :, 0], kh_recv.at[slot])
        high, low = split(hy[slot].reshape(COLS, COLS))
        wnear[slot, 0] = high
        wnear[slot, 1] = low

    def split_c(which, q):
        high, low = split(cbuf[which, rows(q)])
        xb[which, 0, rows(q)] = high
        xb[which, 1, rows(q)] = low

    for slot in ORDER:
        if slot < 8:
            split_own(slot)
    for q in range(CH):
        split_c(0, q)

    ready = []

    def advance(upto):
        while len(ready) < upto:
            at = len(ready)
            for lead, stage in ((2, spread_x), (1, spread_core), (0, split_near)):
                low = 0 if at == 0 else at + lead
                for position in range(low, min(at + lead + 1, len(ORDER))):
                    stage(ORDER[position])
            ready.append(at)

    def product(which, weights, q):
        high, low = xb[which, 0, rows(q)], xb[which, 1, rows(q)]
        return dot(high, weights[0]) + dot(high, weights[1]) + dot(low, weights[0])

    def partial(q, d):
        total = product(0, wown.at[d], q)
        if d == 0:
            return total + product(1, wnear.at[0], q) + product(2, wnear.at[8], q)
        return total + product(jnp.where(inside(d), 1, 2), wnear.at[d], q)

    def lengths(q):
        return (4, 3) if q % 2 == 0 else (3, 4)

    def step_of(q, s):
        if s == 0:
            for which in (1, 2):
                arrived(cbuf.at[which, rows(q)], yc_recv.at[which - 1, q])
                split_c(which, q)
        need = {0: 3, 1: 5, 2: 7, 3: 7, 4: 9}[s]
        advance(need)
        for way, length in zip((1, -1), lengths(q)):
            ring, send, recv, device = (
                (plus, zp_send, zp_recv, z_above) if way == 1 else (minus, zm_send, zm_recv, z_below)
            )
            if s >= length:
                continue
            value = partial(q, (way * (length - s)) % NZ)
            if s == 0:
                first[q, (1 - way) // 2] = value
                source = first.at[q, (1 - way) // 2]
            else:
                arrived(ring.at[q, s - 1], recv.at[q, s - 1])
                ring[q, s - 1] = ring[q, s - 1] + value
                source = ring.at[q, s - 1]
            remote(source, ring.at[q, s], send.at[q, s], recv.at[q, s], device)

    def finish(q):
        advance(9)
        value = partial(q, 0)
        up, down = lengths(q)
        arrived(plus.at[q, up - 1], zp_recv.at[q, up - 1])
        arrived(minus.at[q, down - 1], zm_recv.at[q, down - 1])
        final[q] = value + plus[q, up - 1] + minus[q, down - 1]
        half, part = q // 2, q % 2
        stays = (c // 2 == r) & (c % 2 == half)
        target = mirrored.at[c % 2, part]

        @pl.when(stays)
        def _():
            pltpu.make_async_copy(final.at[q], target, m_recv.at[c % 2, part]).start()

        @pl.when(jnp.logical_not(stays))
        def _():
            pltpu.make_async_remote_copy(
                src_ref=final.at[q], dst_ref=target, send_sem=m_send.at[q], recv_sem=m_recv.at[c % 2, part],
                device_id=(c // 2, 2 * r + half), device_id_type=MESH,
            ).start()

    for slot in range(STAGGER * (CH - 1) + 5):
        for q in range(CH):
            s = slot - STAGGER * q
            if 0 <= s < 4:
                step_of(q, s)
            elif s == 4:
                finish(q)

    for half in range(2):
        for part in range(2):
            arrived(mirrored.at[half, part], m_recv.at[half, part])
            turned = mirrored[half, part].T
            for piece in range(2):
                q = 2 * half + piece
                out_ref[rows(q), part * BS:(part + 1) * BS] = (
                    final[q, :, part * BS:(part + 1) * BS] + turned[piece * QR:(piece + 1) * QR]
                )
    for copy in sends:
        copy.wait_send()
    for q in range(CH):
        @pl.when(jnp.logical_not((c // 2 == r) & (c % 2 == q // 2)))
        def _():
            arrived(final.at[q], m_send.at[q])


def offsets_of(block_columns):
    per_device = block_columns.shape[0]
    blocks = per_device * lax.axis_size("col")
    first = lax.axis_index("col") * per_device
    own = first + jnp.arange(per_device, dtype=jnp.int32)[:, None, None]
    offset = (block_columns[:, None, :] - own + blocks // 2) % blocks - blocks // 2
    asked = jnp.arange(OFFS, dtype=jnp.int32)[None, :, None] - 17
    hit = offset == asked
    where = jnp.sum(jnp.where(hit, jnp.arange(K, dtype=jnp.int32)[None, None, :], 0), axis=2)
    return where, jnp.any(hit, axis=2).astype(jnp.float32)


def local(ci_coeffs, h_blocks, block_columns):
    where, flag = offsets_of(block_columns)
    f32, bf16 = jnp.float32, jnp.bfloat16
    dma = pltpu.SemaphoreType.DMA
    return pl.pallas_call(
        kernel,
        out_shape=jax.ShapeDtypeStruct((ROWS, COLS), f32),
        in_specs=[
            pl.BlockSpec(memory_space=pltpu.SMEM),
            pl.BlockSpec(memory_space=pltpu.SMEM),
            pl.BlockSpec(memory_space=pl.ANY),
            pl.BlockSpec(memory_space=pl.ANY),
        ],
        out_specs=pl.BlockSpec(memory_space=pltpu.VMEM),
        scratch_shapes=[
            pltpu.VMEM((3, ROWS, COLS), f32),
            pltpu.VMEM((2, K, BS, BS), f32),
            pltpu.VMEM((17, 4, 2, 32, COLS), f32),
            pltpu.VMEM((9, 4, 2, 32, COLS), f32),
            pltpu.VMEM((8, 2, COLS, COLS), bf16),
            pltpu.VMEM((9, 2, COLS, COLS), bf16),
            pltpu.VMEM((3, 2, ROWS, COLS), bf16),
            pltpu.VMEM((CH, 2, QR, COLS), f32),
            pltpu.VMEM((CH, 4, QR, COLS), f32),
            pltpu.VMEM((CH, 4, QR, COLS), f32),
            pltpu.VMEM((CH, QR, COLS), f32),
            pltpu.VMEM((2, 2, QR, COLS), f32),
            dma((2,)),
            dma((2, CH)), dma((2, CH)),
            dma((9,)), dma((9,)),
            dma((9, 3)), dma((9, 3)),
            dma((9,)), dma((9,)),
            dma((CH, 4)), dma((CH, 4)),
            dma((CH, 4)), dma((CH, 4)),
            dma((CH,)), dma((2, 2)),
        ],
        compiler_params=pltpu.CompilerParams(
            collective_id=0, has_side_effects=True, vmem_limit_bytes=48 * 2**20
        ),
        cost_estimate=pl.CostEstimate(flops=7 * 10**9, bytes_accessed=5 * 2**20, transcendentals=0),
    )(where, flag, ci_coeffs, h_blocks)


def solution(mesh):
    return jax.shard_map(
        local,
        mesh=mesh,
        in_specs=(P("row", "col"), P("col", None, None, None), P("col", None)),
        out_specs=P("row", "col"),
        check_vma=False,
    )
```

time: 482 us -> 137 us (0.28)
  the two profiles are of different devices: /device:TPU:1 before, /device:TPU:98 now
where the time goes in v1:
time: 137 us
  Pallas kernels  132 us (96%)
  local copies, waits for them, and re-layouts  3.72 us (3%)
    pallas_call x1, Pallas kernels, local(): pl.pallas_call(kernel, out_shape=jax.ShapeDtypeStruct((ROWS, COLS), f32),...  132 us
    unnamed x5, local copies, waits for them, and re-layouts  3.72 us

profile of v1, /device:TPU:98, one launch (start us, length us, event | category | flops | bytes accessed | tf_op | source)
XLA Modules:
  0.0 137.2 jit_solution(1693839852947173603)
XLA Ops:
  0.0 0.8 fusion.1
  0.8 0.1 compare_reduce_fusion
  0.9 0.1 fusion.where_ref
  1.0 0.0 copy-start
  1.0 1.9 %copy-done = f32[2,24,128,128]{3,2,1,0:T(8,128)S(1)} copy-done((f32[2,24,128,128]{3,2,1,0:T(8,128)S(1)}, f32[2,24,128,128]{3,2,1,0:T(8,128)}, u32[]{:S(2)}) %copy-start) | copy-done | bytes 3145752
  2.8 0.0 copy-start.1
  2.9 1.0 copy-done.1
  3.9 132.5 %shard_map.37 = f32[512,256]{1,0:T(8,128)S(1)} custom-call(s32[2,36]{1,0:T(2,128)S(1)} %fusion.where_ref, f32[2,36]{1,0:T(2,128)S(1)} %convert_element_type.3.flag_ref, f32[512,256]{1,0:T(8,128)S(1)} %copy-done.1, f32[2,24,128,128]{3,2,1,0:T(8,128)S(1)} %copy-done), custom_call_target="tpu_custom_call" | custom-call | flops 7000000000 | bytes 5242880 | tf_op jit(solution)/shard_map/pallas_call | solution.py:270
  136.4 0.8 copy.5
  (3 shorter events, 0.0 us)
Async XLA Ops:
  1.0 1.9 %copy-start = (f32[2,24,128,128]{3,2,1,0:T(8,128)S(1)}, f32[2,24,128,128]{3,2,1,0:T(8,128)}, u32[]{:S(2)}) copy-start(f32[2,24,128,128]{3,2,1,0:T(8,128)} %h_hbm.1) | copy-start | bytes 9437188
  2.8 1.0 copy-start.1

commit v2 on v1

--- a/solution.py
+++ b/solution.py
@@ -8,6 +8,7 @@
 NX, NYL, NZ = 4, 4, 8
 BS = 128
 K = 24
+STAGGER = 1
 CH = 4
 ROWS = 512
 COLS = 256
@@ -15,7 +16,8 @@
 OFFS = 36
 MESH = pl.DeviceIdType.MESH
 ORDER = (4, 3, 5, 2, 6, 1, 7, 0, 8)
-STAGGER = 1
+PLACE = {d: p for p, d in enumerate(ORDER)}
+BATCHES = ((0, 3), (3, 5), (5, 9))
 
 
 def split(value):
@@ -30,9 +32,9 @@
 
 def kernel(
     where_ref, flag_ref, c_hbm, h_hbm, out_ref,
-    cbuf, hraw, placed, hy, wown, wnear, xb, first, plus, minus, final, mirrored,
+    cbuf, hraw, placed, hy, wown, wnear, xb, first, plus, minus, final, via, mirrored,
     loc_sem, yc_send, yc_recv, yh_send, yh_recv, xh_send, xh_recv, kh_send, kh_recv,
-    zp_send, zp_recv, zm_send, zm_recv, m_send, m_recv,
+    zp_send, zp_recv, zm_send, zm_recv, m_send, m_recv, v_send, v_recv,
 ):
     r = lax.axis_index("row")
     c = lax.axis_index("col")
@@ -54,7 +56,17 @@
     z_below = (r, y_lo * NZ + (z + NZ - 1) % NZ)
     sibling = (y_hi * 8 + x * 2 + 1 - core, c)
     peers = [along_x(step) for step in (1, 2, 3)]
-    on_diagonal = (c // 2 == r).astype(jnp.int32)
+
+    def beside(row):
+        return row + 6 - 4 * ((row // 2) % NX)
+
+    neighbour = (beside(r), c)
+    straight = [(c // 2, 2 * r + half) for half in range(2)]
+    onward = [(c // 2, 2 * beside(r) + half) for half in range(2)]
+    sources = straight + [(beside(c // 2), 2 * r + half) for half in range(2)]
+
+    def elsewhere(device):
+        return (device[0] != r) | (device[1] != c)
 
     get_c = pltpu.make_async_copy(c_hbm, cbuf.at[0], loc_sem.at[0])
     get_h = pltpu.make_async_copy(h_hbm, hraw, loc_sem.at[1])
@@ -65,13 +77,16 @@
     fixed = [col_above, col_below, y_above, y_below, z_above, z_below, sibling] + peers
     for device in fixed:
         pl.semaphore_signal(barrier, inc=1, device_id=device, device_id_type=MESH)
-    for half in range(2):
-        @pl.when(jnp.logical_not((c // 2 == r) & (c % 2 == half)))
+    for device in sources:
+        @pl.when(elsewhere(device))
         def _():
-            pl.semaphore_signal(barrier, inc=1, device_id=(c // 2, 2 * r + half), device_id_type=MESH)
+            pl.semaphore_signal(barrier, inc=1, device_id=device, device_id_type=MESH)
+    replies = len(fixed)
+    for device in straight + onward:
+        replies = replies + elsewhere(device).astype(jnp.int32)
     get_c.wait()
     get_h.wait()
-    pl.semaphore_wait(barrier, len(fixed) + 2 - on_diagonal)
+    pl.semaphore_wait(barrier, replies)
 
     sends = []
 
@@ -82,6 +97,22 @@
         )
         copy.start()
         sends.append(copy)
+
+    routed = []
+
+    def route(src, dst, send_sem, recv_sem, device):
+        @pl.when(jnp.logical_not(elsewhere(device)))
+        def _():
+            pltpu.make_async_copy(src, dst, recv_sem).start()
+
+        @pl.when(elsewhere(device))
+        def _():
+            pltpu.make_async_remote_copy(
+                src_ref=src, dst_ref=dst, send_sem=send_sem, recv_sem=recv_sem,
+                device_id=device, device_id_type=MESH,
+            ).start()
+
+        routed.append((src, send_sem, elsewhere(device)))
 
     def arrived(ref, sem):
         pltpu.make_async_copy(ref, ref, sem).wait()
@@ -111,7 +142,8 @@
         else:
             index = jnp.where(inside(slot), slot, slot + 8)
             device = tuple(jnp.where(inside(slot), b, a) for a, b in zip(y_above, y_below))
-        remote(placed.at[index, x, core], hy.at[slot, x, core], yh_send.at[slot], yh_recv.at[slot], device)
+        p = PLACE[slot]
+        remote(placed.at[index, x, core], hy.at[p, x, core], yh_send.at[p], yh_recv.at[p], device)
 
     send_c(0)
     for slot in ORDER:
@@ -121,18 +153,21 @@
             place(slot)
             place(slot + 8)
         send_h(slot)
-    for q in range(1, CH):
-        send_c(q)
-
-    def spread_x(slot):
-        arrived(hy.at[slot, x, core], yh_recv.at[slot])
+    def batch(b):
+        return pl.ds(BATCHES[b][0], BATCHES[b][1] - BATCHES[b][0])
+
+    def spread_x(b):
+        for p in range(*BATCHES[b]):
+            arrived(hy.at[p, x, core], yh_recv.at[p])
         for step in range(3):
-            remote(hy.at[slot, x, core], hy.at[slot, x, core], xh_send.at[slot, step], xh_recv.at[slot, step], peers[step])
-
-    def spread_core(slot):
+            piece = hy.at[batch(b), x, core]
+            remote(piece, piece, xh_send.at[b, step], xh_recv.at[b, step], peers[step])
+
+    def spread_core(b):
         for step in range(3):
-            arrived(hy.at[slot, 0, 0], xh_recv.at[slot, step])
-        remote(hy.at[slot, :, core], hy.at[slot, :, core], kh_send.at[slot], kh_recv.at[slot], sibling)
+            arrived(hy.at[batch(b), 0, 0], xh_recv.at[b, step])
+        piece = hy.at[batch(b), :, core]
+        remote(piece, piece, kh_send.at[b], kh_recv.at[b], sibling)
 
     def split_own(d):
         index = 8 if d == 0 else jnp.where(inside(d), d + 8, d)
@@ -140,11 +175,12 @@
         wown[d, 0] = high
         wown[d, 1] = low
 
-    def split_near(slot):
-        arrived(hy.at[slot, :, 0], kh_recv.at[slot])
-        high, low = split(hy[slot].reshape(COLS, COLS))
-        wnear[slot, 0] = high
-        wnear[slot, 1] = low
+    def split_near(b):
+        arrived(hy.at[batch(b), :, 0], kh_recv.at[b])
+        for p in range(*BATCHES[b]):
+            high, low = split(hy[p].reshape(COLS, COLS))
+            wnear[p, 0] = high
+            wnear[p, 1] = low
 
     def split_c(which, q):
         high, low = split(cbuf[which, rows(q)])
@@ -157,16 +193,16 @@
     for q in range(CH):
         split_c(0, q)
 
-    ready = []
+    tasks = [
+        [(spread_x, 0), (send_c, 1), (spread_x, 1), (spread_core, 0), (spread_x, 2), (spread_core, 1), (split_near, 0)],
+        [(split_near, 1), (spread_core, 2)],
+        [(split_near, 2)],
+    ]
 
     def advance(upto):
-        while len(ready) < upto:
-            at = len(ready)
-            for lead, stage in ((2, spread_x), (1, spread_core), (0, split_near)):
-                low = 0 if at == 0 else at + lead
-                for position in range(low, min(at + lead + 1, len(ORDER))):
-                    stage(ORDER[position])
-            ready.append(at)
+        while len(tasks) > 3 - upto:
+            for stage, b in tasks.pop(0):
+                stage(b)
 
     def product(which, weights, q):
         high, low = xb[which, 0, rows(q)], xb[which, 1, rows(q)]
@@ -175,19 +211,20 @@
     def partial(q, d):
         total = product(0, wown.at[d], q)
         if d == 0:
-            return total + product(1, wnear.at[0], q) + product(2, wnear.at[8], q)
-        return total + product(jnp.where(inside(d), 1, 2), wnear.at[d], q)
+            return total + product(1, wnear.at[PLACE[0]], q) + product(2, wnear.at[PLACE[8]], q)
+        return total + product(jnp.where(inside(d), 1, 2), wnear.at[PLACE[d]], q)
 
     def lengths(q):
         return (4, 3) if q % 2 == 0 else (3, 4)
 
     def step_of(q, s):
+        advance(min(s + 1, 3))
         if s == 0:
             for which in (1, 2):
                 arrived(cbuf.at[which, rows(q)], yc_recv.at[which - 1, q])
                 split_c(which, q)
-        need = {0: 3, 1: 5, 2: 7, 3: 7, 4: 9}[s]
-        advance(need)
+            if q + 2 < CH:
+                send_c(q + 2)
         for way, length in zip((1, -1), lengths(q)):
             ring, send, recv, device = (
                 (plus, zp_send, zp_recv, z_above) if way == 1 else (minus, zm_send, zm_recv, z_below)
@@ -205,50 +242,55 @@
             remote(source, ring.at[q, s], send.at[q, s], recv.at[q, s], device)
 
     def finish(q):
-        advance(9)
+        advance(3)
         value = partial(q, 0)
         up, down = lengths(q)
         arrived(plus.at[q, up - 1], zp_recv.at[q, up - 1])
         arrived(minus.at[q, down - 1], zm_recv.at[q, down - 1])
-        final[q] = value + plus[q, up - 1] + minus[q, down - 1]
-        half, part = q // 2, q % 2
-        stays = (c // 2 == r) & (c % 2 == half)
-        target = mirrored.at[c % 2, part]
-
-        @pl.when(stays)
-        def _():
-            pltpu.make_async_copy(final.at[q], target, m_recv.at[c % 2, part]).start()
-
-        @pl.when(jnp.logical_not(stays))
-        def _():
-            pltpu.make_async_remote_copy(
-                src_ref=final.at[q], dst_ref=target, send_sem=m_send.at[q], recv_sem=m_recv.at[c % 2, part],
-                device_id=(c // 2, 2 * r + half), device_id_type=MESH,
-            ).start()
-
-    for slot in range(STAGGER * (CH - 1) + 5):
+        final[rows(q)] = value + plus[q, up - 1] + minus[q, down - 1]
+
+    def part_rows(part):
+        return pl.ds(part * BS, BS)
+
+    def mirror_out(m):
+        half, part = m // 2, m % 2
+        src = final.at[part_rows(m)]
+        if part == 0:
+            remote(src, via.at[half], m_send.at[m], v_recv.at[half], neighbour)
+        else:
+            route(src, mirrored.at[c % 2, part_rows(part)], m_send.at[m], m_recv.at[c % 2, part], straight[half])
+
+    def mirror_on(m):
+        half, part = m // 2, m % 2
+        if part == 0:
+            arrived(via.at[half], v_recv.at[half])
+            route(via.at[half], mirrored.at[c % 2, part_rows(part)], v_send.at[half], m_recv.at[c % 2, part], onward[half])
+
+    group = CH // 4
+    for slot in range(STAGGER * (CH - 1) + 6):
         for q in range(CH):
             s = slot - STAGGER * q
             if 0 <= s < 4:
                 step_of(q, s)
             elif s == 4:
                 finish(q)
+                if q % group == group - 1:
+                    mirror_out(q // group)
+            elif s == 5 and q % group == group - 1:
+                mirror_on(q // group)
 
     for half in range(2):
         for part in range(2):
-            arrived(mirrored.at[half, part], m_recv.at[half, part])
-            turned = mirrored[half, part].T
-            for piece in range(2):
-                q = 2 * half + piece
-                out_ref[rows(q), part * BS:(part + 1) * BS] = (
-                    final[q, :, part * BS:(part + 1) * BS] + turned[piece * QR:(piece + 1) * QR]
-                )
+            arrived(mirrored.at[half, part_rows(part)], m_recv.at[half, part])
+            turned = mirrored[half, part_rows(part)].T
+            at = pl.ds(half * COLS, COLS)
+            out_ref[at, part * BS:(part + 1) * BS] = final[at, part * BS:(part + 1) * BS] + turned
     for copy in sends:
         copy.wait_send()
-    for q in range(CH):
-        @pl.when(jnp.logical_not((c // 2 == r) & (c % 2 == q // 2)))
+    for src, send_sem, role in routed:
+        @pl.when(role)
         def _():
-            arrived(final.at[q], m_send.at[q])
+            arrived(src, send_sem)
 
 
 def offsets_of(block_columns):
@@ -273,8 +315,8 @@
         in_specs=[
             pl.BlockSpec(memory_space=pltpu.SMEM),
             pl.BlockSpec(memory_space=pltpu.SMEM),
-            pl.BlockSpec(memory_space=pl.ANY),
-            pl.BlockSpec(memory_space=pl.ANY),
+            pl.BlockSpec(memory_space=pltpu.HBM),
+            pl.BlockSpec(memory_space=pltpu.HBM),
         ],
         out_specs=pl.BlockSpec(memory_space=pltpu.VMEM),
         scratch_shapes=[
@@ -288,19 +330,21 @@
             pltpu.VMEM((CH, 2, QR, COLS), f32),
             pltpu.VMEM((CH, 4, QR, COLS), f32),
             pltpu.VMEM((CH, 4, QR, COLS), f32),
-            pltpu.VMEM((CH, QR, COLS), f32),
-            pltpu.VMEM((2, 2, QR, COLS), f32),
+            pltpu.VMEM((ROWS, COLS), f32),
+            pltpu.VMEM((2, BS, COLS), f32),
+            pltpu.VMEM((2, 2 * BS, COLS), f32),
             dma((2,)),
             dma((2, CH)), dma((2, CH)),
             dma((9,)), dma((9,)),
-            dma((9, 3)), dma((9, 3)),
-            dma((9,)), dma((9,)),
+            dma((3, 3)), dma((3, 3)),
+            dma((3,)), dma((3,)),
             dma((CH, 4)), dma((CH, 4)),
             dma((CH, 4)), dma((CH, 4)),
-            dma((CH,)), dma((2, 2)),
+            dma((4,)), dma((2, 2)),
+            dma((2,)), dma((2,)),
         ],
         compiler_params=pltpu.CompilerParams(
-            collective_id=0, has_side_effects=True, vmem_limit_bytes=48 * 2**20
+            collective_id=0, has_side_effects=True, vmem_limit_bytes=60 * 2**20
         ),
         cost_estimate=pl.CostEstimate(flops=7 * 10**9, bytes_accessed=5 * 2**20, transcendentals=0),
     )(where, flag, ci_coeffs, h_blocks)

time: 137 us -> 115 us (0.84)
  the two profiles are of different devices: /device:TPU:98 before, /device:TPU:106 now
where the time goes in v2:
time: 115 us
  Pallas kernels  111 us (97%)
  other arithmetic  2.1 us (2%)
  local copies, waits for them, and re-layouts  1.87 us (2%)
    pallas_call x1, Pallas kernels, local(): pl.pallas_call(kernel, out_shape=jax.ShapeDtypeStruct((ROWS, COLS), f32),...  111 us

profile of v2, /device:TPU:106, one launch (start us, length us, event | category | flops | bytes accessed | tf_op | source)
XLA Modules:
  0.0 115.2 jit_solution(1684021220121919306)
XLA Ops:
  0.0 0.8 fusion.1
  0.8 0.1 compare_reduce_fusion
  0.9 0.7 fusion.where_ref
  1.5 0.6 convert_element_type.3.flag_ref
  2.1 111.2 %shard_map.37 = f32[512,256]{1,0:T(8,128)} custom-call(s32[2,36]{1,0:T(2,128)} %fusion.where_ref, f32[2,36]{1,0:T(2,128)} %convert_element_type.3.flag_ref, f32[512,256]{1,0:T(8,128)} %c_hbm.1, f32[2,24,128,128]{3,2,1,0:T(8,128)} %h_hbm.1), custom_call_target="tpu_custom_call" | custom-call | flops 7000000000 | bytes 5242880 | tf_op jit(solution)/shard_map/pallas_call | solution.py:312
  113.3 1.9 %copy.5 = f32[512,256]{1,0:T(8,128)} copy(f32[512,256]{1,0:T(8,128)} %shard_map.37) | data formatting | bytes 1048576
  (2 shorter events, 0.0 us)

commit v3 on v2

--- a/solution.py
+++ b/solution.py
@@ -13,6 +13,8 @@
 ROWS = 512
 COLS = 256
 QR = ROWS // CH
+SUB = 2
+SR = QR // SUB
 OFFS = 36
 MESH = pl.DeviceIdType.MESH
 ORDER = (4, 3, 5, 2, 6, 1, 7, 0, 8)
@@ -32,7 +34,7 @@
 
 def kernel(
     where_ref, flag_ref, c_hbm, h_hbm, out_ref,
-    cbuf, hraw, placed, hy, wown, wnear, xb, first, plus, minus, final, via, mirrored,
+    cbuf, hraw, placed, hy, wown, wnear, xb, sums, plus, minus, final, via, mirrored,
     loc_sem, yc_send, yc_recv, yh_send, yh_recv, xh_send, xh_recv, kh_send, kh_recv,
     zp_send, zp_recv, zm_send, zm_recv, m_send, m_recv, v_send, v_recv,
 ):
@@ -145,7 +147,6 @@
         p = PLACE[slot]
         remote(placed.at[index, x, core], hy.at[p, x, core], yh_send.at[p], yh_recv.at[p], device)
 
-    send_c(0)
     for slot in ORDER:
         if slot == 8:
             place(16)
@@ -153,6 +154,8 @@
             place(slot)
             place(slot + 8)
         send_h(slot)
+        if slot == ORDER[2]:
+            send_c(0)
     def batch(b):
         return pl.ds(BATCHES[b][0], BATCHES[b][1] - BATCHES[b][0])
 
@@ -214,57 +217,70 @@
             return total + product(1, wnear.at[PLACE[0]], q) + product(2, wnear.at[PLACE[8]], q)
         return total + product(jnp.where(inside(d), 1, 2), wnear.at[PLACE[d]], q)
 
+    def compute(g, targets):
+        for d in targets:
+            sums[d, rows(g)] = partial(g, d)
+
     def lengths(q):
         return (4, 3) if q % 2 == 0 else (3, 4)
 
-    def step_of(q, s):
-        advance(min(s + 1, 3))
+    def piece_rows(q):
+        return pl.ds(q * SR, SR)
+
+    def step_of(g, s):
         if s == 0:
+            advance(1)
             for which in (1, 2):
-                arrived(cbuf.at[which, rows(q)], yc_recv.at[which - 1, q])
-                split_c(which, q)
-            if q + 2 < CH:
-                send_c(q + 2)
-        for way, length in zip((1, -1), lengths(q)):
-            ring, send, recv, device = (
-                (plus, zp_send, zp_recv, z_above) if way == 1 else (minus, zm_send, zm_recv, z_below)
-            )
-            if s >= length:
-                continue
-            value = partial(q, (way * (length - s)) % NZ)
-            if s == 0:
-                first[q, (1 - way) // 2] = value
-                source = first.at[q, (1 - way) // 2]
-            else:
-                arrived(ring.at[q, s - 1], recv.at[q, s - 1])
-                ring[q, s - 1] = ring[q, s - 1] + value
-                source = ring.at[q, s - 1]
-            remote(source, ring.at[q, s], send.at[q, s], recv.at[q, s], device)
-
-    def finish(q):
-        advance(3)
-        value = partial(q, 0)
-        up, down = lengths(q)
-        arrived(plus.at[q, up - 1], zp_recv.at[q, up - 1])
-        arrived(minus.at[q, down - 1], zm_recv.at[q, down - 1])
-        final[rows(q)] = value + plus[q, up - 1] + minus[q, down - 1]
+                arrived(cbuf.at[which, rows(g)], yc_recv.at[which - 1, g])
+                split_c(which, g)
+            if g + 2 < CH:
+                send_c(g + 2)
+            compute(g, (4, 5, 3))
+        for q in range(SUB * g, SUB * g + SUB):
+            for way, length in zip((1, -1), lengths(q)):
+                ring, send, recv, device = (
+                    (plus, zp_send, zp_recv, z_above) if way == 1 else (minus, zm_send, zm_recv, z_below)
+                )
+                if s >= length:
+                    continue
+                d = (way * (length - s)) % NZ
+                if s == 0:
+                    source = sums.at[d, piece_rows(q)]
+                else:
+                    arrived(ring.at[q, s - 1], recv.at[q, s - 1])
+                    ring[q, s - 1] = ring[q, s - 1] + sums[d, piece_rows(q)]
+                    source = ring.at[q, s - 1]
+                remote(source, ring.at[q, s], send.at[q, s], recv.at[q, s], device)
+        if s == 0:
+            advance(2)
+            compute(g, (2, 6))
+        if s == 1:
+            advance(3)
+            compute(g, (1, 7, 0))
+
+    def finish(g):
+        for q in range(SUB * g, SUB * g + SUB):
+            up, down = lengths(q)
+            arrived(plus.at[q, up - 1], zp_recv.at[q, up - 1])
+            arrived(minus.at[q, down - 1], zm_recv.at[q, down - 1])
+            final[piece_rows(q)] = sums[0, piece_rows(q)] + plus[q, up - 1] + minus[q, down - 1]
 
     def part_rows(part):
         return pl.ds(part * BS, BS)
 
+    def split_rows(part, way):
+        return pl.ds(part * BS + way * (BS // 2), BS // 2)
+
     def mirror_out(m):
         half, part = m // 2, m % 2
-        src = final.at[part_rows(m)]
-        if part == 0:
-            remote(src, via.at[half], m_send.at[m], v_recv.at[half], neighbour)
-        else:
-            route(src, mirrored.at[c % 2, part_rows(part)], m_send.at[m], m_recv.at[c % 2, part], straight[half])
+        remote(final.at[split_rows(m, 0)], via.at[m], m_send.at[m, 0], v_recv.at[m], neighbour)
+        route(final.at[split_rows(m, 1)], mirrored.at[c % 2, split_rows(part, 1)], m_send.at[m, 1],
+              m_recv.at[c % 2, part, 1], straight[half])
 
     def mirror_on(m):
         half, part = m // 2, m % 2
-        if part == 0:
-            arrived(via.at[half], v_recv.at[half])
-            route(via.at[half], mirrored.at[c % 2, part_rows(part)], v_send.at[half], m_recv.at[c % 2, part], onward[half])
+        arrived(via.at[m], v_recv.at[m])
+        route(via.at[m], mirrored.at[c % 2, split_rows(part, 0)], v_send.at[m], m_recv.at[c % 2, part, 0], onward[half])
 
     group = CH // 4
     for slot in range(STAGGER * (CH - 1) + 6):
@@ -281,7 +297,8 @@
 
     for half in range(2):
         for part in range(2):
-            arrived(mirrored.at[half, part_rows(part)], m_recv.at[half, part])
+            for way in range(2):
+                arrived(mirrored.at[half, split_rows(part, way)], m_recv.at[half, part, way])
             turned = mirrored[half, part_rows(part)].T
             at = pl.ds(half * COLS, COLS)
             out_ref[at, part * BS:(part + 1) * BS] = final[at, part * BS:(part + 1) * BS] + turned
@@ -298,7 +315,7 @@
     blocks = per_device * lax.axis_size("col")
     first = lax.axis_index("col") * per_device
     own = first + jnp.arange(per_device, dtype=jnp.int32)[:, None, None]
-    offset = (block_columns[:, None, :] - own + blocks // 2) % blocks - blocks // 2
+    offset = ((block_columns[:, None, :] - own + blocks // 2) & (blocks - 1)) - blocks // 2
     asked = jnp.arange(OFFS, dtype=jnp.int32)[None, :, None] - 17
     hit = offset == asked
     where = jnp.sum(jnp.where(hit, jnp.arange(K, dtype=jnp.int32)[None, None, :], 0), axis=2)
@@ -327,21 +344,21 @@
             pltpu.VMEM((8, 2, COLS, COLS), bf16),
             pltpu.VMEM((9, 2, COLS, COLS), bf16),
             pltpu.VMEM((3, 2, ROWS, COLS), bf16),
-            pltpu.VMEM((CH, 2, QR, COLS), f32),
-            pltpu.VMEM((CH, 4, QR, COLS), f32),
-            pltpu.VMEM((CH, 4, QR, COLS), f32),
+            pltpu.VMEM((NZ, ROWS, COLS), f32),
+            pltpu.VMEM((CH * SUB, 4, SR, COLS), f32),
+            pltpu.VMEM((CH * SUB, 4, SR, COLS), f32),
             pltpu.VMEM((ROWS, COLS), f32),
-            pltpu.VMEM((2, BS, COLS), f32),
+            pltpu.VMEM((4, BS // 2, COLS), f32),
             pltpu.VMEM((2, 2 * BS, COLS), f32),
             dma((2,)),
             dma((2, CH)), dma((2, CH)),
             dma((9,)), dma((9,)),
             dma((3, 3)), dma((3, 3)),
             dma((3,)), dma((3,)),
-            dma((CH, 4)), dma((CH, 4)),
-            dma((CH, 4)), dma((CH, 4)),
-            dma((4,)), dma((2, 2)),
-            dma((2,)), dma((2,)),
+            dma((CH * SUB, 4)), dma((CH * SUB, 4)),
+            dma((CH * SUB, 4)), dma((CH * SUB, 4)),
+            dma((4, 2)), dma((2, 2, 2)),
+            dma((4,)), dma((4,)),
         ],
         compiler_params=pltpu.CompilerParams(
             collective_id=0, has_side_effects=True, vmem_limit_bytes=60 * 2**20

time: 115 us -> 113 us (0.983)
  the two profiles are of different devices: /device:TPU:106 before, /device:TPU:80 now
where the time goes in v3:
time: 113 us; the launch traced here: 112 us
  Pallas kernels  108 us (96%)
  other arithmetic  2.1 us (2%)
  local copies, waits for them, and re-layouts  1.87 us (2%)
    pallas_call x1, Pallas kernels, local(): pl.pallas_call(kernel, out_shape=jax.ShapeDtypeStruct((ROWS, COLS), f32),...  108 us

profile of v3, /device:TPU:80, one launch (start us, length us, event | category | flops | bytes accessed | tf_op | source)
XLA Modules:
  0.0 112.3 jit_solution(9389621258066329234)
XLA Ops:
  0.0 0.8 and_add_fusion
  0.8 0.1 compare_reduce_fusion
  0.9 0.7 fusion.where_ref
  1.5 0.6 convert_element_type.3.flag_ref
  2.1 108.4 %shard_map.37 = f32[512,256]{1,0:T(8,128)} custom-call(s32[2,36]{1,0:T(2,128)} %fusion.where_ref, f32[2,36]{1,0:T(2,128)} %convert_element_type.3.flag_ref, f32[512,256]{1,0:T(8,128)} %c_hbm.1, f32[2,24,128,128]{3,2,1,0:T(8,128)} %h_hbm.1), custom_call_target="tpu_custom_call" | custom-call | flops 7000000000 | bytes 5242880 | tf_op jit(solution)/shard_map/pallas_call | solution.py:329
  110.5 1.9 %copy.5 = f32[512,256]{1,0:T(8,128)} copy(f32[512,256]{1,0:T(8,128)} %shard_map.37) | data formatting | bytes 1048576
  (2 shorter events, 0.0 us)

commit v4 on v3

--- a/solution.py
+++ b/solution.py
@@ -88,6 +88,16 @@
         replies = replies + elsewhere(device).astype(jnp.int32)
     get_c.wait()
     get_h.wait()
+    def place(index):
+        for j in range(2):
+            for e in range(2):
+                at = 2 * (index - 8) + e - j + 17
+                block = hraw[j, where_ref[j, at]] * flag_ref[j, at]
+                placed[index, 2 * j:2 * j + 2, :, :, e * BS:(e + 1) * BS] = block.reshape(2, 2, 32, BS)
+
+    for slot in ORDER[:3]:
+        place(slot)
+        place(slot + 8)
     pl.semaphore_wait(barrier, replies)
 
     sends = []
@@ -125,13 +135,6 @@
     def send_c(q):
         remote(cbuf.at[0, rows(q)], cbuf.at[2, rows(q)], yc_send.at[0, q], yc_recv.at[1, q], col_above)
         remote(cbuf.at[0, rows(q)], cbuf.at[1, rows(q)], yc_send.at[1, q], yc_recv.at[0, q], col_below)
-
-    def place(index):
-        for j in range(2):
-            for e in range(2):
-                at = 2 * (index - 8) + e - j + 17
-                block = hraw[j, where_ref[j, at]] * flag_ref[j, at]
-                placed[index, 2 * j:2 * j + 2, :, :, e * BS:(e + 1) * BS] = block.reshape(2, 2, 32, BS)
 
     def inside(d):
         return z + d < NZ
@@ -150,7 +153,7 @@
     for slot in ORDER:
         if slot == 8:
             place(16)
-        else:
+        elif slot not in ORDER[:3]:
             place(slot)
             place(slot + 8)
         send_h(slot)

time: 113 us -> 112 us (level)
  no operation moved by 1% of the time
where the time goes in v4:
time: 112 us
  Pallas kernels  108 us (96%)
  other arithmetic  2.1 us (2%)
  local copies, waits for them, and re-layouts  1.87 us (2%)
    pallas_call x1, Pallas kernels, local(): pl.pallas_call(kernel, out_shape=jax.ShapeDtypeStruct((ROWS, COLS), f32),...  108 us

profile of v4, /device:TPU:80, one launch (start us, length us, event | category | flops | bytes accessed | tf_op | source)
XLA Modules:
  0.0 112.2 jit_solution(8846000358610366251)
XLA Ops:
  0.0 0.8 and_add_fusion
  0.8 0.1 compare_reduce_fusion
  0.9 0.7 fusion.where_ref
  1.5 0.6 convert_element_type.3.flag_ref
  2.1 108.3 %shard_map.37 = f32[512,256]{1,0:T(8,128)} custom-call(s32[2,36]{1,0:T(2,128)} %fusion.where_ref, f32[2,36]{1,0:T(2,128)} %convert_element_type.3.flag_ref, f32[512,256]{1,0:T(8,128)} %c_hbm.1, f32[2,24,128,128]{3,2,1,0:T(8,128)} %h_hbm.1), custom_call_target="tpu_custom_call" | custom-call | flops 7000000000 | bytes 5242880 | tf_op jit(solution)/shard_map/pallas_call | solution.py:332
  110.4 1.9 %copy.5 = f32[512,256]{1,0:T(8,128)} copy(f32[512,256]{1,0:T(8,128)} %shard_map.37) | data formatting | bytes 1048576
  (2 shorter events, 0.0 us)
